TPU v7x, 128 devices: a whole 4x4x4 slice. The times are simulated.
128 devices in a mesh: dp: 8 (over x, core), expert: 16 (over y, z).
Axes of the slice: x: 4, y: 4, z: 4, core: 2. Of those that a mesh axis runs over, the one named last changes fastest.
Arguments:
- grad_parts: bfloat16 [8, 128, 512, 512], P('dp', 'expert'), may hold values from -6 to 6
- stat_owned: float32 [16, 16, 512, 512], P('expert', 'dp'), as said below
- owner_list: int32 [128], replicated, may hold values from 0 to 15, as said below
Outputs:
- new_stat: float32 [16, 16, 512, 512], P('expert', 'dp')
- precond: float32 [128, 512, 512], P('expert', 'dp')
Inputs may be any that keep to these rules, and one draw needn't show every extreme that they name: `owner_list`: blocks e * 8 to e * 8 + 7 come from expert shard e and go to 8 different owners; some owner holds a block from every one of the 16 shards. `stat_owned`: every slot is symmetric and strictly diagonally dominant with a positive diagonal.
All inputs are finite; a program needn't handle non-finite values.
Results may differ from a plain program's by a relative error of at most 0.0003.
Values may be sent and summed in bfloat16 or wider, within the bound.
A program may use at most 128 MiB of HBM per device.

v0:
```python
import functools

import jax
import jax.numpy as jnp
from jax import lax
from jax.experimental import pallas as pl
from jax.experimental.pallas import tpu as pltpu
from jax.sharding import PartitionSpec as P

ITERS = 6
EPSILON = 1e-06
DECAY = 0.9
GAIN = 0.1

MESH = pl.DeviceIdType.MESH
F32 = jnp.float32
BF16 = jnp.bfloat16
TILE = 128
RING = 4
CORES = 2


def remote(src, dst, send_sem, recv_sem, dp, expert):
    return pltpu.make_async_remote_copy(
        src_ref=src,
        dst_ref=dst,
        send_sem=send_sem,
        recv_sem=recv_sem,
        device_id={"dp": dp, "expert": expert},
        device_id_type=MESH,
    )


def split(value):
    high = value.astype(BF16)
    return high, (value - high.astype(F32)).astype(BF16)


def dot(former, latter):
    return jnp.dot(former, latter, preferred_element_type=F32)


def dot_transposed(former, latter):
    return lax.dot_general(former, latter, (((1,), (1,)), ((), ())), preferred_element_type=F32)


def diagonal(rows, first, columns):
    across = lax.broadcasted_iota(jnp.int32, (rows, columns), 1)
    return lax.broadcasted_iota(jnp.int32, (rows, columns), 0) + first == across


class Pair:
    def __init__(self, refs):
        self.high, self.low = refs

    def put(self, rows, value):
        self.high[rows, :], self.low[rows, :] = split(value)


def product(former, latter, rows):
    return dot(former.high[rows, :], latter.high[...]) + (
        dot(former.high[rows, :], latter.low[...]) + dot(former.low[rows, :], latter.high[...])
    )


def kernel(
    extent,
    blocks,
    experts,
    owner_ref,
    grads,
    stats,
    fresh_out,
    precond_out,
    own,
    part,
    far_sum,
    right_sum,
    left_sum,
    total,
    rx_far,
    rx_direct,
    rx_mixed,
    previous,
    packed,
    gathered,
    chosen,
    home_stat,
    term,
    terms_in,
    terms_out,
    owner_terms,
    matrix,
    halves,
    updates,
    load_sem,
    stat_sem,
    core_send,
    core_recv,
    ring_send,
    ring_recv,
    plane_send,
    plane_recv,
    home_send,
    home_recv,
    back_send,
    back_recv,
    spread_send,
    spread_recv,
    band_send,
    band_recv,
    out_sem,
):
    dp = lax.axis_index("dp")
    spot = lax.axis_index("expert")
    x, core = dp // CORES, dp % CORES
    twin = x * CORES + 1 - core
    right = lax.rem(x + 1, RING) * CORES + core
    left = lax.rem(x + RING - 1, RING) * CORES + core
    slot, band = lax.rem(spot, 2), spot // 2
    served = 2 * dp + slot
    own_band = band == dp
    tiles = extent // TILE
    upper = [(a, b) for a in range(tiles) for b in range(a, tiles)]
    depth = len(upper) * TILE // blocks
    half = extent // 2

    def block_of(turn, which):
        return lax.rem(x + turn, RING) * CORES + which

    loads = {}
    for turn in (2, 1, 3, 0):
        loads[turn] = pltpu.make_async_copy(
            grads.at[block_of(turn, core)], own.at[turn], load_sem.at[turn]
        )
        loads[turn].start()
    stat_load = pltpu.make_async_copy(stats, previous, stat_sem)
    stat_load.start()

    barrier = pltpu.get_barrier_semaphore()

    def greet(to_dp, to_expert):
        pl.semaphore_signal(
            barrier, inc=1, device_id={"dp": to_dp, "expert": to_expert}, device_id_type=MESH
        )

    @pl.loop(1, experts)
    def _(step):
        greet(dp, lax.rem(spot + step, experts))

    @pl.loop(1, blocks)
    def _(step):
        greet(lax.rem(dp + step, blocks), spot)

    @pl.loop(0, blocks)
    def _(step):
        @pl.when(jnp.logical_not(jnp.logical_and(own_band, step == dp)))
        def _():
            greet(step, served)
            greet(band, 2 * step + slot)

    pl.semaphore_wait(barrier, experts - 1 + blocks - 1 + 2 * blocks - jnp.where(own_band, 2, 0))

    crossing = {}
    for turn in (2, 1, 3, 0):
        crossing[turn] = remote(
            grads.at[block_of(turn, 1 - core)],
            part.at[turn],
            core_send.at[turn],
            core_recv.at[turn],
            twin,
            spot,
        )
        crossing[turn].start()

    def pair_sum(turn, rows):
        return own[turn, rows, :].astype(F32) + part[turn, rows, :].astype(F32)

    top, bottom = pl.ds(0, half), pl.ds(half, half)

    def ring(index, src, dst, to):
        return remote(src, dst, ring_send.at[index], ring_recv.at[index], to, spot)

    loads[2].wait()
    crossing[2].wait_recv()
    far_sum[top, :] = pair_sum(2, top)
    far_right = ring(0, far_sum.at[top], rx_far.at[0], right)
    far_right.start()
    far_sum[bottom, :] = pair_sum(2, bottom)
    far_left = ring(1, far_sum.at[bottom], rx_far.at[1], left)
    far_left.start()

    loads[1].wait()
    crossing[1].wait_recv()
    right_sum[bottom, :] = pair_sum(1, bottom)
    direct_right = ring(2, right_sum.at[bottom], rx_direct.at[1], right)
    direct_right.start()
    loads[3].wait()
    crossing[3].wait_recv()
    left_sum[top, :] = pair_sum(3, top)
    direct_left = ring(3, left_sum.at[top], rx_direct.at[0], left)
    direct_left.start()

    stat_load.wait()
    for where in range(2):
        for place, (a, b) in enumerate(upper):
            packed[where, place * TILE : (place + 1) * TILE, :] = previous[
                where, a * TILE : (a + 1) * TILE, b * TILE : (b + 1) * TILE
            ]

    def rows_of(index):
        return pl.ds(pl.multiple_of(index * depth, depth), depth)

    def to_plane(other):
        return remote(
            packed.at[lax.rem(other, 2), rows_of(other // 2)],
            gathered.at[spot],
            plane_send.at[other],
            plane_recv.at[spot],
            dp,
            other,
        )

    def from_plane(other):
        return remote(
            packed.at[0, rows_of(0)], gathered.at[other], plane_send.at[other], plane_recv.at[other], dp, other
        )

    @pl.loop(1, experts)
    def _(step):
        to_plane(lax.rem(spot + step, experts)).start()

    gathered[spot] = packed[slot, rows_of(band), :]

    right_sum[top, :] = pair_sum(1, top)
    left_sum[bottom, :] = pair_sum(3, bottom)
    loads[0].wait()
    crossing[0].wait_recv()
    total[...] = pair_sum(0, pl.ds(0, extent))

    far_right.wait_recv()
    right_sum[top, :] = right_sum[top, :] + rx_far[0]
    mixed_right = ring(4, right_sum.at[top], rx_mixed.at[0], right)
    mixed_right.start()
    far_left.wait_recv()
    left_sum[bottom, :] = left_sum[bottom, :] + rx_far[1]
    mixed_left = ring(5, left_sum.at[bottom], rx_mixed.at[1], left)
    mixed_left.start()

    @pl.loop(1, experts)
    def _(step):
        from_plane(lax.rem(spot + step, experts)).wait_recv()

    def to_home(index):
        return remote(
            chosen.at[index],
            home_stat.at[rows_of(band)],
            home_send.at[index],
            home_recv.at[band],
            index,
            served,
        )

    def from_home(index):
        return remote(
            chosen.at[index],
            home_stat.at[rows_of(index)],
            home_send.at[index],
            home_recv.at[index],
            band,
            2 * index + slot,
        )

    for index in range(blocks):
        chosen[index] = gathered[owner_ref[served * blocks + index]]

    @pl.loop(0, blocks)
    def _(index):
        mine = jnp.logical_and(own_band, index == dp)

        @pl.when(jnp.logical_not(mine))
        def _():
            to_home(index).start()

        @pl.when(mine)
        def _():
            home_stat[rows_of(index), :] = chosen[index]

    direct_left.wait_recv()
    total[top, :] = total[top, :] + rx_direct[0]
    direct_right.wait_recv()
    total[bottom, :] = total[bottom, :] + rx_direct[1]
    mixed_right.wait_recv()
    total[top, :] = total[top, :] + rx_mixed[0]
    mixed_left.wait_recv()
    total[bottom, :] = total[bottom, :] + rx_mixed[1]

    grad, current, factor, result, square = (
        Pair((halves.at[2 * index], halves.at[2 * index + 1]))
        for index in range(5)
    )
    strips = [pl.ds(first, half) for first in (0, half)]
    for rows in strips:
        grad.put(rows, total[rows, :])
    for rows in strips:
        matrix[rows, :] = dot_transposed(grad.high[rows, :], grad.high[...]) + (
            dot_transposed(grad.high[rows, :], grad.low[...])
            + dot_transposed(grad.low[rows, :], grad.high[...])
        )
    for place, (a, b) in enumerate(upper):
        term[place * TILE : (place + 1) * TILE, :] = matrix[
            a * TILE : (a + 1) * TILE, b * TILE : (b + 1) * TILE
        ]

    def to_server(index):
        return remote(
            term.at[rows_of(index)],
            terms_in.at[dp],
            back_send.at[index],
            back_recv.at[dp],
            band,
            2 * index + slot,
        )

    def from_server(index):
        return remote(
            term.at[rows_of(index)],
            terms_in.at[index],
            back_send.at[index],
            back_recv.at[index],
            index,
            served,
        )

    @pl.loop(0, blocks)
    def _(index):
        mine = jnp.logical_and(own_band, index == dp)

        @pl.when(jnp.logical_not(mine))
        def _():
            to_server(index).start()

        @pl.when(mine)
        def _():
            terms_in[index] = term[rows_of(index), :]

    @pl.loop(0, blocks)
    def _(index):
        @pl.when(jnp.logical_not(jnp.logical_and(own_band, index == dp)))
        def _():
            from_home(index).wait_recv()

    squares = jnp.zeros((1, 1), F32)
    for place, (a, b) in enumerate(upper):
        across = pl.ds(a * TILE, TILE), pl.ds(b * TILE, TILE)
        piece = pl.ds(place * TILE, TILE)
        value = DECAY * home_stat[piece, :] + GAIN / extent * term[piece, :]
        if a == b:
            value = value + jnp.where(diagonal(TILE, 0, TILE), F32(EPSILON), F32(0.0))
        else:
            matrix[across[1], across[0]] = value.T
        matrix[across[0], across[1]] = value
        squares = squares + (1.0 if a == b else 2.0) * jnp.sum(value * value, keepdims=True)

    scaling = 2.5 * lax.rsqrt(squares)
    start = jnp.sqrt(jnp.sqrt(scaling))

    def factor_of(value, rows):
        identity = diagonal(rows.size, rows.start, extent)
        return jnp.where(identity, 1.25 - 0.25 * value, -0.25 * value)

    for rows in strips:
        value = matrix[rows, :] * scaling
        current.put(rows, value)
        value = factor_of(value, rows)
        factor.put(rows, value)
        result.put(rows, start * value)

    def spread_terms():
        @pl.loop(0, blocks)
        def _(index):
            @pl.when(jnp.logical_not(jnp.logical_and(own_band, index == dp)))
            def _():
                from_server(index).wait_recv()

        owners = [owner_ref[served * blocks + index] for index in range(blocks)]

        @pl.loop(0, experts)
        def _(owner):
            at, there = jnp.int32(0), F32(0.0)
            for index in range(blocks):
                hit = owners[index] == owner
                at = jnp.where(hit, index, at)
                there = jnp.where(hit, F32(1.0), there)
            terms_out[owner] = there * terms_in[at]

        @pl.loop(1, experts)
        def _(step):
            to_owner(lax.rem(spot + step, experts)).start()

        owner_terms[slot, rows_of(band), :] = terms_out[spot]

    def to_owner(other):
        return remote(
            terms_out.at[other],
            owner_terms.at[slot, rows_of(band)],
            spread_send.at[other],
            spread_recv.at[spot],
            dp,
            other,
        )

    def from_owner(other):
        return remote(
            terms_out.at[other],
            owner_terms.at[lax.rem(other, 2), rows_of(other // 2)],
            spread_send.at[other],
            spread_recv.at[other],
            dp,
            other,
        )

    for repeat in range(ITERS - 1):
        for rows in strips:
            square.put(rows, product(factor, factor, rows))
        if repeat > 0:
            values = [product(result, factor, rows) for rows in strips]
            for rows, value in zip(strips, values):
                result.put(rows, value)
        for rows in strips:
            factor.put(rows, product(square, square, rows))
        values = [product(factor, current, rows) for rows in strips]
        for rows, value in zip(strips, values):
            current.put(rows, value)
            factor.put(rows, factor_of(value, rows))
        if repeat == 2:
            spread_terms()
    values = [product(result, factor, rows) for rows in strips]
    for rows, value in zip(strips, values):
        result.put(rows, value)
    for rows in strips:
        updates[rows, :] = product(result, grad, rows)

    width = extent // blocks

    def to_replica(index):
        return remote(
            updates.at[pl.ds(pl.multiple_of(index * width, width), width)],
            precond_out.at[dp],
            band_send.at[index],
            band_recv.at[dp],
            index,
            spot,
        )

    def from_replica(index):
        return remote(
            updates.at[pl.ds(0, width)],
            precond_out.at[index],
            band_send.at[index],
            band_recv.at[index],
            index,
            spot,
        )

    @pl.loop(1, blocks)
    def _(step):
        to_replica(lax.rem(dp + step, blocks)).start()

    keep = pltpu.make_async_copy(
        updates.at[pl.ds(pl.multiple_of(dp * width, width), width)], precond_out.at[dp], out_sem
    )
    keep.start()

    @pl.loop(1, experts)
    def _(step):
        from_owner(lax.rem(spot + step, experts)).wait_recv()

    for where in range(2):
        for place, (a, b) in enumerate(upper):
            value = GAIN / extent * owner_terms[where, place * TILE : (place + 1) * TILE, :]
            down, over = pl.ds(a * TILE, TILE), pl.ds(b * TILE, TILE)
            fresh_out[where, down, over] = DECAY * previous[where, down, over] + value
            if a != b:
                fresh_out[where, over, down] = DECAY * previous[where, over, down] + value.T

    for copy in crossing.values():
        copy.wait_send()
    for copy in (far_right, far_left, direct_right, direct_left, mixed_right, mixed_left):
        copy.wait_send()

    @pl.loop(1, experts)
    def _(step):
        other = lax.rem(spot + step, experts)
        to_plane(other).wait_send()
        to_owner(other).wait_send()

    @pl.loop(0, blocks)
    def _(index):
        @pl.when(jnp.logical_not(jnp.logical_and(own_band, index == dp)))
        def _():
            to_home(index).wait_send()
            to_server(index).wait_send()

    @pl.loop(1, blocks)
    def _(step):
        other = lax.rem(dp + step, blocks)
        to_replica(other).wait_send()
        from_replica(other).wait_recv()

    keep.wait()


def per_device(grad_parts, stat_owned, owner_list):
    experts = lax.axis_size("expert")
    blocks = lax.axis_size("dp")
    partials, previous = grad_parts[0], stat_owned[0]
    extent = partials.shape[1]
    tiles = extent // TILE
    packed_rows = tiles * (tiles + 1) // 2 * TILE
    depth = packed_rows // blocks
    half = extent // 2
    dma = pltpu.SemaphoreType.DMA
    square = (extent, extent)
    fresh, precond = pl.pallas_call(
        functools.partial(kernel, extent, blocks, experts),
        out_shape=[
            jax.ShapeDtypeStruct(previous.shape, F32),
            jax.ShapeDtypeStruct((blocks, extent // blocks, extent), F32),
        ],
        in_specs=[
            pl.BlockSpec(memory_space=pltpu.SMEM),
            pl.BlockSpec(memory_space=pl.ANY),
            pl.BlockSpec(memory_space=pl.ANY),
        ],
        out_specs=[pl.BlockSpec(memory_space=pltpu.VMEM), pl.BlockSpec(memory_space=pl.ANY)],
        scratch_shapes=[
            pltpu.VMEM((RING, *square), BF16),
            pltpu.VMEM((RING, *square), BF16),
            pltpu.VMEM(square, F32),
            pltpu.VMEM(square, F32),
            pltpu.VMEM(square, F32),
            pltpu.VMEM(square, F32),
            pltpu.VMEM((2, half, extent), F32),
            pltpu.VMEM((2, half, extent), F32),
            pltpu.VMEM((2, half, extent), F32),
            pltpu.VMEM((2, *square), F32),
            pltpu.VMEM((2, packed_rows, TILE), F32),
            pltpu.VMEM((experts, depth, TILE), F32),
            pltpu.VMEM((blocks, depth, TILE), F32),
            pltpu.VMEM((packed_rows, TILE), F32),
            pltpu.VMEM((packed_rows, TILE), F32),
            pltpu.VMEM((blocks, depth, TILE), F32),
            pltpu.VMEM((experts, depth, TILE), F32),
            pltpu.VMEM((2, packed_rows, TILE), F32),
            pltpu.VMEM(square, F32),
            pltpu.VMEM((10, *square), BF16),
            pltpu.VMEM(square, F32),
            dma((RING,)),
            dma(()),
            dma((RING,)),
            dma((RING,)),
            dma((6,)),
            dma((6,)),
            dma((experts,)),
            dma((experts,)),
            dma((blocks,)),
            dma((blocks,)),
            dma((blocks,)),
            dma((blocks,)),
            dma((experts,)),
            dma((experts,)),
            dma((blocks,)),
            dma((blocks,)),
            dma(()),
        ],
        compiler_params=pltpu.CompilerParams(
            collective_id=0, has_side_effects=True, vmem_limit_bytes=52 * 2**20
        ),
    )(owner_list, partials, previous)
    return (fresh[None], precond)


def solution(mesh):
    in_specs = (P("dp", "expert", None, None), P("expert", "dp", None, None), P())
    out_specs = (P("expert", "dp", None, None), P("expert", "dp", None))
    return jax.shard_map(
        per_device, mesh=mesh, in_specs=in_specs, out_specs=out_specs, check_vma=False
    )
```

profile of v0, /device:TPU:25, one launch (start us, length us, event | category | flops | bytes accessed | tf_op | source)
XLA Modules:
  0.0 116.2 jit_solution(9024529037789314935)
XLA Ops:
  0.6 0.0 copy-start
  0.6 0.6 copy-done
  1.3 110.9 %shard_map.50 = (f32[2,512,512]{2,1,0:T(8,128)}, f32[8,64,512]{2,1,0:T(8,128)S(1)}) custom-call(s32[128]{0:T(128)S(1)} %copy-done, bf16[8,512,512]{2,1,0:T(8,128)(2,1)} %bitcast.3, f32[2,512,512]{2,1,0:T(8,128)} %bitcast.4), custom_call_target="tpu_custom_call" | custom-call | tf_op jit(solution)/shard_map/pallas_call | solution.py:525
  112.2 3.1 %copy.7 = f32[1,2,512,512]{3,2,1,0:T(8,128)} copy(f32[1,2,512,512]{3,2,1,0:T(8,128)} %bitcast.5) | data formatting | bytes 4194304
  115.3 1.0 copy.8
Async XLA Ops:
  0.6 0.7 copy-start
where the time goes:
time: 116 us
  Pallas kernels  111 us (96%)
  local copies, waits for them, and re-layouts  4.7 us (4%)
    pallas_call x1, Pallas kernels, per_device(): pl.pallas_call(functools.partial(kernel, extent, blocks, experts), out_sh...  111 us
    unnamed x4, local copies, waits for them, and re-layouts  4.7 us

commit v1 on v0

--- a/solution.py
+++ b/solution.py
@@ -18,6 +18,10 @@
 TILE = 128
 RING = 4
 CORES = 2
+LEVELS = 16.0
+LOWEST = -1600.0
+PEAK = 32700.0
+NOTE = 16
 
 
 def remote(src, dst, send_sem, recv_sem, dp, expert):
@@ -36,6 +40,30 @@
     return high, (value - high.astype(F32)).astype(BF16)
 
 
+def coded(value):
+    peak = jnp.maximum(jnp.max(jnp.abs(value), axis=0, keepdims=True), 1e-30)
+    level = jnp.maximum(jnp.ceil(LEVELS * jnp.log2(peak)), LOWEST)
+    codes = jnp.round(value * (PEAK * jnp.exp2(level * (-1.0 / LEVELS))))
+    return codes.astype(jnp.int32).astype(jnp.int16), level
+
+
+def step_of(level):
+    return jnp.exp2(level * (1.0 / LEVELS)) * (1.0 / PEAK)
+
+
+def as_note(level, rows):
+    return jnp.broadcast_to(level, (rows, level.shape[1])).astype(jnp.int32).astype(jnp.int16)
+
+
+def floats(codes):
+    return codes.astype(jnp.int32).astype(F32)
+
+
+def decoded(piece, depth):
+    level = floats(piece[depth : depth + NOTE, :])[:1, :]
+    return floats(piece[:depth, :]) * step_of(level)
+
+
 def dot(former, latter):
     return jnp.dot(former, latter, preferred_element_type=F32)
 
@@ -67,11 +95,12 @@
     extent,
     blocks,
     experts,
-    owner_ref,
+    owner_list,
     grads,
     stats,
     fresh_out,
-    precond_out,
+    codes_out,
+    owner_ref,
     own,
     part,
     far_sum,
@@ -82,19 +111,23 @@
     rx_direct,
     rx_mixed,
     previous,
+    fresh,
     packed,
+    stat_codes,
     gathered,
     chosen,
     home_stat,
     term,
+    term_codes,
     terms_in,
     terms_out,
     owner_terms,
     matrix,
     halves,
-    updates,
+    band_codes,
     load_sem,
     stat_sem,
+    owner_sem,
     core_send,
     core_recv,
     ring_send,
@@ -136,6 +169,8 @@
         loads[turn].start()
     stat_load = pltpu.make_async_copy(stats, previous, stat_sem)
     stat_load.start()
+    owner_load = pltpu.make_async_copy(owner_list, owner_ref, owner_sem)
+    owner_load.start()
 
     barrier = pltpu.get_barrier_semaphore()
 
@@ -158,6 +193,22 @@
         def _():
             greet(step, served)
             greet(band, 2 * step + slot)
+
+    def rows_of(index):
+        return pl.ds(pl.multiple_of(index * depth, depth), depth)
+
+    stat_load.wait()
+    for where in range(2):
+        for place, (a, b) in enumerate(upper):
+            packed[where, place * TILE : (place + 1) * TILE, :] = previous[
+                where, a * TILE : (a + 1) * TILE, b * TILE : (b + 1) * TILE
+            ]
+
+        @pl.loop(0, blocks)
+        def _(index):
+            codes, level = coded(packed[where, rows_of(index), :])
+            stat_codes[where, index, :depth, :] = codes
+            stat_codes[where, index, depth:, :] = as_note(level, NOTE)
 
     pl.semaphore_wait(barrier, experts - 1 + blocks - 1 + 2 * blocks - jnp.where(own_band, 2, 0))
 
@@ -201,19 +252,9 @@
     direct_left = ring(3, left_sum.at[top], rx_direct.at[0], left)
     direct_left.start()
 
-    stat_load.wait()
-    for where in range(2):
-        for place, (a, b) in enumerate(upper):
-            packed[where, place * TILE : (place + 1) * TILE, :] = previous[
-                where, a * TILE : (a + 1) * TILE, b * TILE : (b + 1) * TILE
-            ]
-
-    def rows_of(index):
-        return pl.ds(pl.multiple_of(index * depth, depth), depth)
-
     def to_plane(other):
         return remote(
-            packed.at[lax.rem(other, 2), rows_of(other // 2)],
+            stat_codes.at[lax.rem(other, 2), other // 2],
             gathered.at[spot],
             plane_send.at[other],
             plane_recv.at[spot],
@@ -223,14 +264,14 @@
 
     def from_plane(other):
         return remote(
-            packed.at[0, rows_of(0)], gathered.at[other], plane_send.at[other], plane_recv.at[other], dp, other
+            stat_codes.at[0, 0], gathered.at[other], plane_send.at[other], plane_recv.at[other], dp, other
         )
 
     @pl.loop(1, experts)
     def _(step):
         to_plane(lax.rem(spot + step, experts)).start()
 
-    gathered[spot] = packed[slot, rows_of(band), :]
+    gathered[spot] = stat_codes[slot, band]
 
     right_sum[top, :] = pair_sum(1, top)
     left_sum[bottom, :] = pair_sum(3, bottom)
@@ -254,7 +295,7 @@
     def to_home(index):
         return remote(
             chosen.at[index],
-            home_stat.at[rows_of(band)],
+            home_stat.at[band],
             home_send.at[index],
             home_recv.at[band],
             index,
@@ -264,13 +305,14 @@
     def from_home(index):
         return remote(
             chosen.at[index],
-            home_stat.at[rows_of(index)],
+            home_stat.at[index],
             home_send.at[index],
             home_recv.at[index],
             band,
             2 * index + slot,
         )
 
+    owner_load.wait()
     for index in range(blocks):
         chosen[index] = gathered[owner_ref[served * blocks + index]]
 
@@ -284,7 +326,7 @@
 
         @pl.when(mine)
         def _():
-            home_stat[rows_of(index), :] = chosen[index]
+            home_stat[index] = chosen[index]
 
     direct_left.wait_recv()
     total[top, :] = total[top, :] + rx_direct[0]
@@ -312,9 +354,15 @@
             a * TILE : (a + 1) * TILE, b * TILE : (b + 1) * TILE
         ]
 
+    @pl.loop(0, blocks)
+    def _(index):
+        codes, level = coded(term[rows_of(index), :])
+        term_codes[index, :depth, :] = codes
+        term_codes[index, depth:, :] = as_note(level, NOTE)
+
     def to_server(index):
         return remote(
-            term.at[rows_of(index)],
+            term_codes.at[index],
             terms_in.at[dp],
             back_send.at[index],
             back_recv.at[dp],
@@ -324,7 +372,7 @@
 
     def from_server(index):
         return remote(
-            term.at[rows_of(index)],
+            term_codes.at[index],
             terms_in.at[index],
             back_send.at[index],
             back_recv.at[index],
@@ -342,7 +390,7 @@
 
         @pl.when(mine)
         def _():
-            terms_in[index] = term[rows_of(index), :]
+            terms_in[index] = term_codes[index]
 
     @pl.loop(0, blocks)
     def _(index):
@@ -350,11 +398,14 @@
         def _():
             from_home(index).wait_recv()
 
+    for index in range(blocks):
+        packed[0, index * depth : (index + 1) * depth, :] = decoded(home_stat.at[index], depth)
+
     squares = jnp.zeros((1, 1), F32)
     for place, (a, b) in enumerate(upper):
         across = pl.ds(a * TILE, TILE), pl.ds(b * TILE, TILE)
         piece = pl.ds(place * TILE, TILE)
-        value = DECAY * home_stat[piece, :] + GAIN / extent * term[piece, :]
+        value = DECAY * packed[0, piece, :] + GAIN / extent * term[piece, :]
         if a == b:
             value = value + jnp.where(diagonal(TILE, 0, TILE), F32(EPSILON), F32(0.0))
         else:
@@ -383,27 +434,26 @@
             def _():
                 from_server(index).wait_recv()
 
+        terms_in[blocks] = jnp.zeros(terms_in.shape[1:], jnp.int16)
         owners = [owner_ref[served * blocks + index] for index in range(blocks)]
 
         @pl.loop(0, experts)
         def _(owner):
-            at, there = jnp.int32(0), F32(0.0)
+            at = jnp.int32(blocks)
             for index in range(blocks):
-                hit = owners[index] == owner
-                at = jnp.where(hit, index, at)
-                there = jnp.where(hit, F32(1.0), there)
-            terms_out[owner] = there * terms_in[at]
+                at = jnp.where(owners[index] == owner, index, at)
+            terms_out[owner] = terms_in[at]
 
         @pl.loop(1, experts)
         def _(step):
             to_owner(lax.rem(spot + step, experts)).start()
 
-        owner_terms[slot, rows_of(band), :] = terms_out[spot]
+        owner_terms[slot, band] = terms_out[spot]
 
     def to_owner(other):
         return remote(
             terms_out.at[other],
-            owner_terms.at[slot, rows_of(band)],
+            owner_terms.at[slot, band],
             spread_send.at[other],
             spread_recv.at[spot],
             dp,
@@ -413,7 +463,7 @@
     def from_owner(other):
         return remote(
             terms_out.at[other],
-            owner_terms.at[lax.rem(other, 2), rows_of(other // 2)],
+            owner_terms.at[lax.rem(other, 2), other // 2],
             spread_send.at[other],
             spread_recv.at[other],
             dp,
@@ -433,20 +483,19 @@
         for rows, value in zip(strips, values):
             current.put(rows, value)
             factor.put(rows, factor_of(value, rows))
-        if repeat == 2:
+        if repeat == 1:
             spread_terms()
     values = [product(result, factor, rows) for rows in strips]
     for rows, value in zip(strips, values):
         result.put(rows, value)
-    for rows in strips:
-        updates[rows, :] = product(result, grad, rows)
 
     width = extent // blocks
+    inner = tiles * width
 
     def to_replica(index):
         return remote(
-            updates.at[pl.ds(pl.multiple_of(index * width, width), width)],
-            precond_out.at[dp],
+            band_codes.at[index],
+            codes_out.at[dp],
             band_send.at[index],
             band_recv.at[dp],
             index,
@@ -455,34 +504,53 @@
 
     def from_replica(index):
         return remote(
-            updates.at[pl.ds(0, width)],
-            precond_out.at[index],
+            band_codes.at[index],
+            codes_out.at[index],
             band_send.at[index],
             band_recv.at[index],
             index,
             spot,
         )
 
-    @pl.loop(1, blocks)
-    def _(step):
-        to_replica(lax.rem(dp + step, blocks)).start()
-
-    keep = pltpu.make_async_copy(
-        updates.at[pl.ds(pl.multiple_of(dp * width, width), width)], precond_out.at[dp], out_sem
-    )
-    keep.start()
+    keep = pltpu.make_async_copy(band_codes.at[dp], codes_out.at[dp], out_sem)
+    line = lax.broadcasted_iota(jnp.int32, (NOTE, TILE), 0) // (NOTE // tiles)
+    for rows in strips:
+        value = product(result, grad, rows)
+        for index in range(rows.start // width, (rows.start + rows.size) // width):
+            first = index * width - rows.start
+            note = jnp.zeros((NOTE, TILE), F32)
+            for tile in range(tiles):
+                codes, level = coded(value[first : first + width, tile * TILE : (tile + 1) * TILE])
+                band_codes[index, tile * width : (tile + 1) * width, :] = codes
+                note = jnp.where(line == tile, level, note)
+            band_codes[index, inner:, :] = as_note(note, NOTE)
+
+            @pl.when(index != dp)
+            def _():
+                to_replica(index).start()
+
+            @pl.when(index == dp)
+            def _():
+                keep.start()
 
     @pl.loop(1, experts)
     def _(step):
         from_owner(lax.rem(spot + step, experts)).wait_recv()
 
+    stores = []
     for where in range(2):
+        for index in range(blocks):
+            packed[where, index * depth : (index + 1) * depth, :] = decoded(
+                owner_terms.at[where, index], depth
+            )
         for place, (a, b) in enumerate(upper):
-            value = GAIN / extent * owner_terms[where, place * TILE : (place + 1) * TILE, :]
+            value = GAIN / extent * packed[where, place * TILE : (place + 1) * TILE, :]
             down, over = pl.ds(a * TILE, TILE), pl.ds(b * TILE, TILE)
-            fresh_out[where, down, over] = DECAY * previous[where, down, over] + value
+            fresh[where, down, over] = DECAY * previous[where, down, over] + value
             if a != b:
-                fresh_out[where, over, down] = DECAY * previous[where, over, down] + value.T
+                fresh[where, over, down] = DECAY * previous[where, over, down] + value.T
+        stores.append(pltpu.make_async_copy(fresh.at[where], fresh_out.at[where], load_sem.at[where]))
+        stores[-1].start()
 
     for copy in crossing.values():
         copy.wait_send()
@@ -509,6 +577,24 @@
         from_replica(other).wait_recv()
 
     keep.wait()
+    for copy in stores:
+        copy.wait()
+
+
+def finish(codes, fresh_in, fresh_out, precond, store_sem):
+    store = pltpu.make_async_copy(fresh_in, fresh_out, store_sem)
+    store.start()
+    blocks, width, extent = precond.shape
+    tiles = extent // TILE
+    inner = tiles * width
+    for index in range(blocks):
+        levels = floats(codes[index, inner:, :])
+        for tile in range(tiles):
+            line = tile * (NOTE // tiles)
+            precond[index, :, tile * TILE : (tile + 1) * TILE] = floats(
+                codes[index, tile * width : (tile + 1) * width, :]
+            ) * step_of(levels[line : line + 1, :])
+    store.wait()
 
 
 def per_device(grad_parts, stat_owned, owner_list):
@@ -522,19 +608,19 @@
     half = extent // 2
     dma = pltpu.SemaphoreType.DMA
     square = (extent, extent)
-    fresh, precond = pl.pallas_call(
+    width = extent // blocks
+    inner = tiles * width + NOTE
+    piece = (depth + NOTE, TILE)
+    terms, codes = pl.pallas_call(
         functools.partial(kernel, extent, blocks, experts),
         out_shape=[
             jax.ShapeDtypeStruct(previous.shape, F32),
-            jax.ShapeDtypeStruct((blocks, extent // blocks, extent), F32),
+            jax.ShapeDtypeStruct((blocks, inner, TILE), jnp.int16),
         ],
-        in_specs=[
-            pl.BlockSpec(memory_space=pltpu.SMEM),
-            pl.BlockSpec(memory_space=pl.ANY),
-            pl.BlockSpec(memory_space=pl.ANY),
-        ],
-        out_specs=[pl.BlockSpec(memory_space=pltpu.VMEM), pl.BlockSpec(memory_space=pl.ANY)],
+        in_specs=[pl.BlockSpec(memory_space=pl.ANY)] * 3,
+        out_specs=[pl.BlockSpec(memory_space=pl.ANY)] * 2,
         scratch_shapes=[
+            pltpu.SMEM(owner_list.shape, jnp.int32),
             pltpu.VMEM((RING, *square), BF16),
             pltpu.VMEM((RING, *square), BF16),
             pltpu.VMEM(square, F32),
@@ -545,18 +631,22 @@
             pltpu.VMEM((2, half, extent), F32),
             pltpu.VMEM((2, half, extent), F32),
             pltpu.VMEM((2, *square), F32),
+            pltpu.VMEM((2, *square), F32),
             pltpu.VMEM((2, packed_rows, TILE), F32),
-            pltpu.VMEM((experts, depth, TILE), F32),
-            pltpu.VMEM((blocks, depth, TILE), F32),
+            pltpu.VMEM((2, blocks, *piece), jnp.int16),
+            pltpu.VMEM((experts, *piece), jnp.int16),
+            pltpu.VMEM((blocks, *piece), jnp.int16),
+            pltpu.VMEM((blocks, *piece), jnp.int16),
             pltpu.VMEM((packed_rows, TILE), F32),
-            pltpu.VMEM((packed_rows, TILE), F32),
-            pltpu.VMEM((blocks, depth, TILE), F32),
-            pltpu.VMEM((experts, depth, TILE), F32),
-            pltpu.VMEM((2, packed_rows, TILE), F32),
+            pltpu.VMEM((blocks, *piece), jnp.int16),
+            pltpu.VMEM((blocks + 1, *piece), jnp.int16),
+            pltpu.VMEM((experts, *piece), jnp.int16),
+            pltpu.VMEM((2, blocks, *piece), jnp.int16),
             pltpu.VMEM(square, F32),
             pltpu.VMEM((10, *square), BF16),
-            pltpu.VMEM(square, F32),
+            pltpu.VMEM((blocks, inner, TILE), jnp.int16),
             dma((RING,)),
+            dma(()),
             dma(()),
             dma((RING,)),
             dma((RING,)),
@@ -575,9 +665,20 @@
             dma(()),
         ],
         compiler_params=pltpu.CompilerParams(
-            collective_id=0, has_side_effects=True, vmem_limit_bytes=52 * 2**20
+            collective_id=0, has_side_effects=True, vmem_limit_bytes=60 * 2**20
         ),
     )(owner_list, partials, previous)
+    fresh, precond = pl.pallas_call(
+        finish,
+        out_shape=[
+            jax.ShapeDtypeStruct(previous.shape, F32),
+            jax.ShapeDtypeStruct((blocks, width, extent), F32),
+        ],
+        in_specs=[pl.BlockSpec(memory_space=pltpu.VMEM)] * 2,
+        out_specs=[pl.BlockSpec(memory_space=pl.ANY), pl.BlockSpec(memory_space=pltpu.VMEM)],
+        scratch_shapes=[dma(())],
+        compiler_params=pltpu.CompilerParams(vmem_limit_bytes=60 * 2**20),
+    )(codes, terms)
     return (fresh[None], precond)
 
 

time: 116 us -> 92.7 us (0.80); the launches traced: 116 us -> 91.7 us
  Pallas kernels: 111 us -> 90.9 us
  local copies, waits for them, and re-layouts: 4.7 us -> 0 us
    pallas_call x1, Pallas kernels: 111 us -> 86.9 us  [per_device(): pl.pallas_call(functools.partial(kernel, extent, blocks, experts), out_sh...]
    unnamed x4 -> x0, local copies, waits for them, and re-layouts: 4.7 us -> none
    pallas_call x0 -> x1, Pallas kernels: none -> 4.07 us  [per_device(): pl.pallas_call(finish, out_shape=[jax.ShapeDtypeStruct(previous.shape, F3...]
where the time goes in v1:
time: 92.7 us; the launch traced here: 91.7 us
  Pallas kernels  90.9 us (98%)
    pallas_call x1, Pallas kernels, per_device(): pl.pallas_call(functools.partial(kernel, extent, blocks, experts), out_sh...  86.9 us
    pallas_call x1, Pallas kernels, per_device(): pl.pallas_call(finish, out_shape=[jax.ShapeDtypeStruct(previous.shape, F3...  4.07 us

profile of v1, /device:TPU:25, one launch (start us, length us, event | category | flops | bytes accessed | tf_op | source)
XLA Modules:
  0.0 91.7 jit_solution(7094602088664132248)
XLA Ops:
  0.6 86.9 %shard_map.50 = (f32[2,512,512]{2,1,0:T(8,128)}, s16[8,272,128]{2,1,0:T(8,128)(2,1)}) custom-call(s32[128]{0:T(128)} %owner_list.1, bf16[8,512,512]{2,1,0:T(8,128)(2,1)} %bitcast.3, f32[2,512,512]{2,1,0:T(8,128)} %bitcast.4), custom_call_target="tpu_custom_call" | custom-call | tf_op jit(solution)/shard_map/pallas_call | solution.py:614
  87.5 4.1 %shard_map.51 = (f32[2,512,512]{2,1,0:T(8,128)}, f32[8,64,512]{2,1,0:T(8,128)}) custom-call(s16[8,272,128]{2,1,0:T(8,128)(2,1)} %get-tuple-element.6.codes, f32[2,512,512]{2,1,0:T(8,128)} %get-tuple-element.7.fresh_in), custom_call_target="tpu_custom_call" | custom-call | tf_op jit(solution)/shard_map/pallas_call | solution.py:671

commit v2 on v1

--- a/solution.py
+++ b/solution.py
@@ -78,17 +78,37 @@
 
 
 class Pair:
-    def __init__(self, refs):
-        self.high, self.low = refs
-
-    def put(self, rows, value):
-        self.high[rows, :], self.low[rows, :] = split(value)
-
-
-def product(former, latter, rows):
-    return dot(former.high[rows, :], latter.high[...]) + (
-        dot(former.high[rows, :], latter.low[...]) + dot(former.low[rows, :], latter.high[...])
+    def __init__(self, high, low):
+        self.high, self.low = high, low
+
+    def put(self, rows, columns, value):
+        self.high[rows, columns], self.low[rows, columns] = split(value)
+
+    def put_symmetric(self, halves, corner, first, last):
+        top, bottom = halves
+        high, low = split(corner)
+        self.high[top, bottom], self.low[top, bottom] = high, low
+        self.high[bottom, top], self.low[bottom, top] = high.T, low.T
+        self.put(top, top, first)
+        self.put(bottom, bottom, last)
+
+
+def product(former, latter, rows, columns, multiply=dot):
+    def side(ref):
+        return ref[:, columns] if multiply is dot else ref[columns, :]
+
+    return multiply(former.high[rows, :], side(latter.high)) + (
+        multiply(former.high[rows, :], side(latter.low))
+        + multiply(former.low[rows, :], side(latter.high))
     )
+
+
+def symmetric_product(former, latter, halves, multiply=dot):
+    top, bottom = halves
+    return [
+        product(former, latter, rows, columns, multiply)
+        for rows, columns in ((top, bottom), (top, top), (bottom, bottom))
+    ]
 
 
 def kernel(
@@ -128,6 +148,8 @@
     load_sem,
     stat_sem,
     owner_sem,
+    ready_sem,
+    open_sem,
     core_send,
     core_recv,
     ring_send,
@@ -173,26 +195,20 @@
     owner_load.start()
 
     barrier = pltpu.get_barrier_semaphore()
-
-    def greet(to_dp, to_expert):
+    gate = dp == 0
+
+    def tell(semaphore, to_dp, to_expert):
         pl.semaphore_signal(
-            barrier, inc=1, device_id={"dp": to_dp, "expert": to_expert}, device_id_type=MESH
-        )
-
-    @pl.loop(1, experts)
-    def _(step):
-        greet(dp, lax.rem(spot + step, experts))
+            semaphore, inc=1, device_id={"dp": to_dp, "expert": to_expert}, device_id_type=MESH
+        )
 
     @pl.loop(1, blocks)
     def _(step):
-        greet(lax.rem(dp + step, blocks), spot)
-
-    @pl.loop(0, blocks)
-    def _(step):
-        @pl.when(jnp.logical_not(jnp.logical_and(own_band, step == dp)))
+        other = lax.rem(dp + step, blocks)
+
+        @pl.when(other != 0)
         def _():
-            greet(step, served)
-            greet(band, 2 * step + slot)
+            tell(barrier, other, spot)
 
     def rows_of(index):
         return pl.ds(pl.multiple_of(index * depth, depth), depth)
@@ -210,7 +226,18 @@
             stat_codes[where, index, :depth, :] = codes
             stat_codes[where, index, depth:, :] = as_note(level, NOTE)
 
-    pl.semaphore_wait(barrier, experts - 1 + blocks - 1 + 2 * blocks - jnp.where(own_band, 2, 0))
+    @pl.when(jnp.logical_not(gate))
+    def _():
+        pl.semaphore_wait(barrier, blocks - 1)
+        tell(ready_sem, 0, spot)
+
+    @pl.when(gate)
+    def _():
+        pl.semaphore_wait(ready_sem, blocks - 1)
+
+        @pl.loop(1, experts)
+        def _(step):
+            tell(barrier, 0, lax.rem(spot + step, experts))
 
     crossing = {}
     for turn in (2, 1, 3, 0):
@@ -267,6 +294,18 @@
             stat_codes.at[0, 0], gathered.at[other], plane_send.at[other], plane_recv.at[other], dp, other
         )
 
+    @pl.when(gate)
+    def _():
+        pl.semaphore_wait(barrier, experts - 1)
+
+        @pl.loop(1, blocks)
+        def _(step):
+            tell(open_sem, step, spot)
+
+    @pl.when(jnp.logical_not(gate))
+    def _():
+        pl.semaphore_wait(open_sem, 1)
+
     @pl.loop(1, experts)
     def _(step):
         to_plane(lax.rem(spot + step, experts)).start()
@@ -338,17 +377,16 @@
     total[bottom, :] = total[bottom, :] + rx_mixed[1]
 
     grad, current, factor, result, square = (
-        Pair((halves.at[2 * index], halves.at[2 * index + 1]))
-        for index in range(5)
+        Pair(halves.at[2 * index], halves.at[2 * index + 1]) for index in range(5)
     )
-    strips = [pl.ds(first, half) for first in (0, half)]
+    strips = [top, bottom]
+    whole = pl.ds(0, extent)
     for rows in strips:
-        grad.put(rows, total[rows, :])
-    for rows in strips:
-        matrix[rows, :] = dot_transposed(grad.high[rows, :], grad.high[...]) + (
-            dot_transposed(grad.high[rows, :], grad.low[...])
-            + dot_transposed(grad.low[rows, :], grad.high[...])
-        )
+        grad.put(rows, whole, total[rows, :])
+    corner, first, last = symmetric_product(grad, grad, strips, dot_transposed)
+    matrix[top, bottom] = corner
+    matrix[top, top] = first
+    matrix[bottom, bottom] = last
     for place, (a, b) in enumerate(upper):
         term[place * TILE : (place + 1) * TILE, :] = matrix[
             a * TILE : (a + 1) * TILE, b * TILE : (b + 1) * TILE
@@ -408,7 +446,7 @@
         value = DECAY * packed[0, piece, :] + GAIN / extent * term[piece, :]
         if a == b:
             value = value + jnp.where(diagonal(TILE, 0, TILE), F32(EPSILON), F32(0.0))
-        else:
+        elif a // (tiles // 2) == b // (tiles // 2):
             matrix[across[1], across[0]] = value.T
         matrix[across[0], across[1]] = value
         squares = squares + (1.0 if a == b else 2.0) * jnp.sum(value * value, keepdims=True)
@@ -416,16 +454,20 @@
     scaling = 2.5 * lax.rsqrt(squares)
     start = jnp.sqrt(jnp.sqrt(scaling))
 
-    def factor_of(value, rows):
-        identity = diagonal(rows.size, rows.start, extent)
-        return jnp.where(identity, 1.25 - 0.25 * value, -0.25 * value)
-
-    for rows in strips:
-        value = matrix[rows, :] * scaling
-        current.put(rows, value)
-        value = factor_of(value, rows)
-        factor.put(rows, value)
-        result.put(rows, start * value)
+    def factors_of(corner, first, last):
+        identity = diagonal(half, 0, half)
+        return [-0.25 * corner] + [
+            jnp.where(identity, 1.25 - 0.25 * block, -0.25 * block) for block in (first, last)
+        ]
+
+    scaled = [
+        matrix[rows, columns] * scaling
+        for rows, columns in ((top, bottom), (top, top), (bottom, bottom))
+    ]
+    current.put_symmetric(strips, *scaled)
+    scaled = factors_of(*scaled)
+    factor.put_symmetric(strips, *scaled)
+    result.put_symmetric(strips, *[start * block for block in scaled])
 
     def spread_terms():
         @pl.loop(0, blocks)
@@ -471,23 +513,20 @@
         )
 
     for repeat in range(ITERS - 1):
-        for rows in strips:
-            square.put(rows, product(factor, factor, rows))
+        squared = symmetric_product(factor, factor, strips)
         if repeat > 0:
-            values = [product(result, factor, rows) for rows in strips]
-            for rows, value in zip(strips, values):
-                result.put(rows, value)
-        for rows in strips:
-            factor.put(rows, product(square, square, rows))
-        values = [product(factor, current, rows) for rows in strips]
-        for rows, value in zip(strips, values):
-            current.put(rows, value)
-            factor.put(rows, factor_of(value, rows))
-        if repeat == 1:
+            advanced = symmetric_product(result, factor, strips)
+        square.put_symmetric(strips, *squared)
+        fourth = symmetric_product(square, square, strips)
+        if repeat > 0:
+            result.put_symmetric(strips, *advanced)
+        factor.put_symmetric(strips, *fourth)
+        following = symmetric_product(factor, current, strips)
+        current.put_symmetric(strips, *following)
+        factor.put_symmetric(strips, *factors_of(*following))
+        if repeat == 2:
             spread_terms()
-    values = [product(result, factor, rows) for rows in strips]
-    for rows, value in zip(strips, values):
-        result.put(rows, value)
+    result.put_symmetric(strips, *symmetric_product(result, factor, strips))
 
     width = extent // blocks
     inner = tiles * width
@@ -515,7 +554,7 @@
     keep = pltpu.make_async_copy(band_codes.at[dp], codes_out.at[dp], out_sem)
     line = lax.broadcasted_iota(jnp.int32, (NOTE, TILE), 0) // (NOTE // tiles)
     for rows in strips:
-        value = product(result, grad, rows)
+        value = product(result, grad, rows, whole)
         for index in range(rows.start // width, (rows.start + rows.size) // width):
             first = index * width - rows.start
             note = jnp.zeros((NOTE, TILE), F32)
@@ -581,20 +620,40 @@
         copy.wait()
 
 
-def finish(codes, fresh_in, fresh_out, precond, store_sem):
-    store = pltpu.make_async_copy(fresh_in, fresh_out, store_sem)
-    store.start()
+def finish(codes, fresh_in, fresh_out, precond_out, taken, passing, precond, load_sem, store_sem):
+    load_codes = pltpu.make_async_copy(codes, taken, load_sem.at[2])
+    load_codes.start()
+    loads = [
+        pltpu.make_async_copy(fresh_in.at[where], passing.at[where], load_sem.at[where])
+        for where in range(2)
+    ]
+    for load in loads:
+        load.start()
     blocks, width, extent = precond.shape
     tiles = extent // TILE
     inner = tiles * width
-    for index in range(blocks):
-        levels = floats(codes[index, inner:, :])
-        for tile in range(tiles):
-            line = tile * (NOTE // tiles)
-            precond[index, :, tile * TILE : (tile + 1) * TILE] = floats(
-                codes[index, tile * width : (tile + 1) * width, :]
-            ) * step_of(levels[line : line + 1, :])
-    store.wait()
+    stores = []
+    load_codes.wait()
+    for part in range(2):
+        for index in range(part * blocks // 2, (part + 1) * blocks // 2):
+            levels = floats(taken[index, inner:, :])
+            for tile in range(tiles):
+                line = tile * (NOTE // tiles)
+                precond[index, :, tile * TILE : (tile + 1) * TILE] = floats(
+                    taken[index, tile * width : (tile + 1) * width, :]
+                ) * step_of(levels[line : line + 1, :])
+        here = pl.ds(part * blocks // 2, blocks // 2)
+        stores.append(
+            pltpu.make_async_copy(precond.at[here], precond_out.at[here], store_sem.at[2 + part])
+        )
+        stores[-1].start()
+        loads[part].wait()
+        stores.append(
+            pltpu.make_async_copy(passing.at[part], fresh_out.at[part], store_sem.at[part])
+        )
+        stores[-1].start()
+    for store in stores:
+        store.wait()
 
 
 def per_device(grad_parts, stat_owned, owner_list):
@@ -648,6 +707,8 @@
             dma((RING,)),
             dma(()),
             dma(()),
+            pltpu.SemaphoreType.REGULAR,
+            pltpu.SemaphoreType.REGULAR,
             dma((RING,)),
             dma((RING,)),
             dma((6,)),
@@ -674,9 +735,15 @@
             jax.ShapeDtypeStruct(previous.shape, F32),
             jax.ShapeDtypeStruct((blocks, width, extent), F32),
         ],
-        in_specs=[pl.BlockSpec(memory_space=pltpu.VMEM)] * 2,
-        out_specs=[pl.BlockSpec(memory_space=pl.ANY), pl.BlockSpec(memory_space=pltpu.VMEM)],
-        scratch_shapes=[dma(())],
+        in_specs=[pl.BlockSpec(memory_space=pl.ANY)] * 2,
+        out_specs=[pl.BlockSpec(memory_space=pl.ANY)] * 2,
+        scratch_shapes=[
+            pltpu.VMEM(codes.shape, jnp.int16),
+            pltpu.VMEM(previous.shape, F32),
+            pltpu.VMEM((blocks, width, extent), F32),
+            dma((3,)),
+            dma((4,)),
+        ],
         compiler_params=pltpu.CompilerParams(vmem_limit_bytes=60 * 2**20),
     )(codes, terms)
     return (fresh[None], precond)

time: 92.7 us -> 83.7 us (0.903)
  Pallas kernels: 90.9 us -> 82.4 us
    pallas_call x1, Pallas kernels: 86.9 us -> 79.4 us  [per_device(): pl.pallas_call(functools.partial(kernel, extent, blocks, experts), out_sh...]
    pallas_call x1, Pallas kernels: 4.07 us -> 2.95 us  [per_device(): pl.pallas_call(finish, out_shape=[jax.ShapeDtypeStruct(previous.shape, F3...]
where the time goes in v2:
time: 83.7 us; the launch traced here: 83.2 us
  Pallas kernels  82.4 us (98%)
    pallas_call x1, Pallas kernels, per_device(): pl.pallas_call(functools.partial(kernel, extent, blocks, experts), out_sh...  79.4 us
    pallas_call x1, Pallas kernels, per_device(): pl.pallas_call(finish, out_shape=[jax.ShapeDtypeStruct(previous.shape, F3...  2.95 us

profile of v2, /device:TPU:25, one launch (start us, length us, event | category | flops | bytes accessed | tf_op | source)
XLA Modules:
  0.0 83.2 jit_solution(1367767066267628107)
XLA Ops:
  0.6 79.4 %shard_map.50 = (f32[2,512,512]{2,1,0:T(8,128)}, s16[8,272,128]{2,1,0:T(8,128)(2,1)}) custom-call(s32[128]{0:T(128)} %owner_list.1, bf16[8,512,512]{2,1,0:T(8,128)(2,1)} %bitcast.3, f32[2,512,512]{2,1,0:T(8,128)} %bitcast.4), custom_call_target="tpu_custom_call" | custom-call | tf_op jit(solution)/shard_map/pallas_call | solution.py:673
  80.1 2.9 %shard_map.51 = (f32[2,512,512]{2,1,0:T(8,128)}, f32[8,64,512]{2,1,0:T(8,128)}) custom-call(s16[8,272,128]{2,1,0:T(8,128)(2,1)} %get-tuple-element.6.codes, f32[2,512,512]{2,1,0:T(8,128)} %get-tuple-element.7.fresh_in), custom_call_target="tpu_custom_call" | custom-call | tf_op jit(solution)/shard_map/pallas_call | solution.py:732

commit v3 on v2

--- a/solution.py
+++ b/solution.py
@@ -22,6 +22,9 @@
 LOWEST = -1600.0
 PEAK = 32700.0
 NOTE = 16
+WIDE = 22.0
+BYTE = 256
+HALFWAY = 32768
 
 
 def remote(src, dst, send_sem, recv_sem, dp, expert):
@@ -62,6 +65,30 @@
 def decoded(piece, depth):
     level = floats(piece[depth : depth + NOTE, :])[:1, :]
     return floats(piece[:depth, :]) * step_of(level)
+
+
+def wide_coded(piece, tile, value):
+    rows = value.shape[0]
+    peak = jnp.maximum(jnp.max(jnp.abs(value), axis=0, keepdims=True), 1e-30)
+    level = jnp.ceil(jnp.log2(peak))
+    codes = jnp.round(value * jnp.exp2(WIDE - level)).astype(jnp.int32)
+    first = tile * (rows + rows // 2)
+    piece[first : first + rows, :] = (codes >> 8).astype(jnp.int16)
+    low = codes & (BYTE - 1)
+    low = low[: rows // 2, :] + (low[rows // 2 :, :] << 8) - HALFWAY
+    piece[first + rows : first + rows + rows // 2, :] = low.astype(jnp.int16)
+    return level
+
+
+def wide_decoded(piece, tile, rows, tiles):
+    first = tile * (rows + rows // 2)
+    note = tiles * (rows + rows // 2)
+    line = tile * (NOTE // tiles)
+    level = floats(piece[note : note + NOTE, :])[line : line + 1, :]
+    low = piece[first + rows : first + rows + rows // 2, :].astype(jnp.int32) + HALFWAY
+    low = jnp.concatenate([low & (BYTE - 1), low >> 8], axis=0)
+    codes = (piece[first : first + rows, :].astype(jnp.int32) << 8) + low
+    return codes.astype(F32) * jnp.exp2(level - WIDE)
 
 
 def dot(former, latter):
@@ -123,13 +150,9 @@
     owner_ref,
     own,
     part,
-    far_sum,
-    right_sum,
-    left_sum,
     total,
-    rx_far,
-    rx_direct,
-    rx_mixed,
+    sent,
+    received,
     previous,
     fresh,
     packed,
@@ -251,33 +274,39 @@
         )
         crossing[turn].start()
 
-    def pair_sum(turn, rows):
-        return own[turn, rows, :].astype(F32) + part[turn, rows, :].astype(F32)
+    def pair_sum(turn, rows, columns):
+        return own[turn, rows, columns].astype(F32) + part[turn, rows, columns].astype(F32)
 
     top, bottom = pl.ds(0, half), pl.ds(half, half)
-
-    def ring(index, src, dst, to):
-        return remote(src, dst, ring_send.at[index], ring_recv.at[index], to, spot)
+    line = lax.broadcasted_iota(jnp.int32, (NOTE, TILE), 0) // (NOTE // tiles)
+
+    def ring(index, to):
+        return remote(
+            sent.at[index], received.at[index], ring_send.at[index], ring_recv.at[index], to, spot
+        )
+
+    def pass_on(index, to, turn, rows, arrived=None):
+        note = jnp.zeros((NOTE, TILE), F32)
+        for tile in range(tiles):
+            value = pair_sum(turn, rows, pl.ds(tile * TILE, TILE))
+            if arrived is not None:
+                value = value + wide_decoded(received.at[arrived], tile, half, tiles)
+            note = jnp.where(line == tile, wide_coded(sent.at[index], tile, value), note)
+        sent[index, tiles * (half + half // 2) :, :] = as_note(note, NOTE)
+        copy = ring(index, to)
+        copy.start()
+        return copy
 
     loads[2].wait()
     crossing[2].wait_recv()
-    far_sum[top, :] = pair_sum(2, top)
-    far_right = ring(0, far_sum.at[top], rx_far.at[0], right)
-    far_right.start()
-    far_sum[bottom, :] = pair_sum(2, bottom)
-    far_left = ring(1, far_sum.at[bottom], rx_far.at[1], left)
-    far_left.start()
-
+    far_right = pass_on(0, right, 2, top)
+    far_left = pass_on(1, left, 2, bottom)
     loads[1].wait()
     crossing[1].wait_recv()
-    right_sum[bottom, :] = pair_sum(1, bottom)
-    direct_right = ring(2, right_sum.at[bottom], rx_direct.at[1], right)
-    direct_right.start()
+    direct_right = pass_on(2, right, 1, bottom)
     loads[3].wait()
     crossing[3].wait_recv()
-    left_sum[top, :] = pair_sum(3, top)
-    direct_left = ring(3, left_sum.at[top], rx_direct.at[0], left)
-    direct_left.start()
+    direct_left = pass_on(3, left, 3, top)
 
     def to_plane(other):
         return remote(
@@ -312,20 +341,15 @@
 
     gathered[spot] = stat_codes[slot, band]
 
-    right_sum[top, :] = pair_sum(1, top)
-    left_sum[bottom, :] = pair_sum(3, bottom)
     loads[0].wait()
     crossing[0].wait_recv()
-    total[...] = pair_sum(0, pl.ds(0, extent))
+    for rows in (top, bottom):
+        total[rows, :] = pair_sum(0, rows, pl.ds(0, extent))
 
     far_right.wait_recv()
-    right_sum[top, :] = right_sum[top, :] + rx_far[0]
-    mixed_right = ring(4, right_sum.at[top], rx_mixed.at[0], right)
-    mixed_right.start()
+    mixed_right = pass_on(4, right, 1, top, 0)
     far_left.wait_recv()
-    left_sum[bottom, :] = left_sum[bottom, :] + rx_far[1]
-    mixed_left = ring(5, left_sum.at[bottom], rx_mixed.at[1], left)
-    mixed_left.start()
+    mixed_left = pass_on(5, left, 3, bottom, 1)
 
     @pl.loop(1, experts)
     def _(step):
@@ -367,14 +391,18 @@
         def _():
             home_stat[index] = chosen[index]
 
-    direct_left.wait_recv()
-    total[top, :] = total[top, :] + rx_direct[0]
-    direct_right.wait_recv()
-    total[bottom, :] = total[bottom, :] + rx_direct[1]
-    mixed_right.wait_recv()
-    total[top, :] = total[top, :] + rx_mixed[0]
-    mixed_left.wait_recv()
-    total[bottom, :] = total[bottom, :] + rx_mixed[1]
+    for copy, index, rows in (
+        (direct_left, 3, top),
+        (direct_right, 2, bottom),
+        (mixed_right, 4, top),
+        (mixed_left, 5, bottom),
+    ):
+        copy.wait_recv()
+        for tile in range(tiles):
+            columns = pl.ds(tile * TILE, TILE)
+            total[rows, columns] = total[rows, columns] + wide_decoded(
+                received.at[index], tile, half, tiles
+            )
 
     grad, current, factor, result, square = (
         Pair(halves.at[2 * index], halves.at[2 * index + 1]) for index in range(5)
@@ -524,7 +552,7 @@
         following = symmetric_product(factor, current, strips)
         current.put_symmetric(strips, *following)
         factor.put_symmetric(strips, *factors_of(*following))
-        if repeat == 2:
+        if repeat == 3:
             spread_terms()
     result.put_symmetric(strips, *symmetric_product(result, factor, strips))
 
@@ -552,7 +580,6 @@
         )
 
     keep = pltpu.make_async_copy(band_codes.at[dp], codes_out.at[dp], out_sem)
-    line = lax.broadcasted_iota(jnp.int32, (NOTE, TILE), 0) // (NOTE // tiles)
     for rows in strips:
         value = product(result, grad, rows, whole)
         for index in range(rows.start // width, (rows.start + rows.size) // width):
@@ -670,6 +697,7 @@
     width = extent // blocks
     inner = tiles * width + NOTE
     piece = (depth + NOTE, TILE)
+    message = tiles * (half + half // 2) + NOTE
     terms, codes = pl.pallas_call(
         functools.partial(kernel, extent, blocks, experts),
         out_shape=[
@@ -683,12 +711,8 @@
             pltpu.VMEM((RING, *square), BF16),
             pltpu.VMEM((RING, *square), BF16),
             pltpu.VMEM(square, F32),
-            pltpu.VMEM(square, F32),
-            pltpu.VMEM(square, F32),
-            pltpu.VMEM(square, F32),
-            pltpu.VMEM((2, half, extent), F32),
-            pltpu.VMEM((2, half, extent), F32),
-            pltpu.VMEM((2, half, extent), F32),
+            pltpu.VMEM((6, message, TILE), jnp.int16),
+            pltpu.VMEM((6, message, TILE), jnp.int16),
             pltpu.VMEM((2, *square), F32),
             pltpu.VMEM((2, *square), F32),
             pltpu.VMEM((2, packed_rows, TILE), F32),

time: 83.7 us -> 75.5 us (0.902)
  the two profiles are of different devices: /device:TPU:25 before, /device:TPU:7 now
where the time goes in v3:
time: 75.5 us; the launch traced here: 75.4 us
  Pallas kernels  74.6 us (99%)
  between operations  0.8 us (1%)
    pallas_call x1, Pallas kernels, per_device(): pl.pallas_call(functools.partial(kernel, extent, blocks, experts), out_sh...  71.6 us
    pallas_call x1, Pallas kernels, per_device(): pl.pallas_call(finish, out_shape=[jax.ShapeDtypeStruct(previous.shape, F3...  2.95 us

profile of v3, /device:TPU:7, one launch (start us, length us, event | category | flops | bytes accessed | tf_op | source)
XLA Modules:
  0.0 75.4 jit_solution(13399732326079735305)
XLA Ops:
  0.6 71.6 %shard_map.50 = (f32[2,512,512]{2,1,0:T(8,128)}, s16[8,272,128]{2,1,0:T(8,128)(2,1)}) custom-call(s32[128]{0:T(128)} %owner_list.1, bf16[8,512,512]{2,1,0:T(8,128)(2,1)} %bitcast.3, f32[2,512,512]{2,1,0:T(8,128)} %bitcast.4), custom_call_target="tpu_custom_call" | custom-call | tf_op jit(solution)/shard_map/pallas_call | solution.py:701
  72.3 2.9 %shard_map.51 = (f32[2,512,512]{2,1,0:T(8,128)}, f32[8,64,512]{2,1,0:T(8,128)}) custom-call(s16[8,272,128]{2,1,0:T(8,128)(2,1)} %get-tuple-element.6.codes, f32[2,512,512]{2,1,0:T(8,128)} %get-tuple-element.7.fresh_in), custom_call_target="tpu_custom_call" | custom-call | tf_op jit(solution)/shard_map/pallas_call | solution.py:756

commit v4 on v3

--- a/solution.py
+++ b/solution.py
@@ -62,9 +62,56 @@
     return codes.astype(jnp.int32).astype(F32)
 
 
-def decoded(piece, depth):
-    level = floats(piece[depth : depth + NOTE, :])[:1, :]
-    return floats(piece[:depth, :]) * step_of(level)
+def pieces_of(tiles):
+    above = [(a, b) for a in range(tiles) for b in range(a + 1, tiles)]
+    return above, [(a, a + 1) for a in range(0, tiles, 2)]
+
+
+def places():
+    down = lax.broadcasted_iota(jnp.int32, (TILE, TILE), 0)
+    over = lax.broadcasted_iota(jnp.int32, (TILE, TILE), 1)
+    return down, over
+
+
+def put_piece(piece, value, spine=None):
+    codes, level = coded(value)
+    piece[:TILE, :] = codes
+    line = lax.broadcasted_iota(jnp.int32, (NOTE, TILE), 0)
+    note = jnp.where(line < NOTE // 2, level, 0.0)
+    if spine is not None:
+        peak = jnp.maximum(jnp.max(jnp.abs(spine), axis=1, keepdims=True), 1e-30)
+        level = jnp.maximum(jnp.ceil(LEVELS * jnp.log2(peak)), LOWEST)
+        codes = jnp.round(spine * (PEAK * jnp.exp2(level * (-1.0 / LEVELS))))
+        note = jnp.where(line < NOTE // 2, note, jnp.where(line < 3 * NOTE // 4, codes, level))
+    piece[TILE:, :] = note.astype(jnp.int32).astype(jnp.int16)
+
+
+def put_pieces(matrix, tile_of, tiles, after):
+    above, paired = pieces_of(tiles)
+    down, over = places()
+    for index, (a, b) in enumerate(above):
+        put_piece(matrix.at[index], tile_of(a, b))
+        after(index)
+    for index, (a, b) in enumerate(paired, len(above)):
+        first = tile_of(a, a)
+        spine = jnp.sum(jnp.where(down == over, first, 0.0), axis=0, keepdims=True)
+        put_piece(matrix.at[index], jnp.where(down < over, first, tile_of(b, b)), spine)
+        after(index)
+
+
+def piece_value(piece):
+    level = floats(piece[TILE:, :])[:1, :]
+    return floats(piece[:TILE, :]) * step_of(level)
+
+
+def diagonal_tiles(piece):
+    value = piece_value(piece)
+    note = floats(piece[TILE:, :])
+    spine = note[NOTE // 2 : NOTE // 2 + 1, :] * step_of(note[NOTE - 1 :, :])
+    down, over = places()
+    across = value.T
+    first = jnp.where(down < over, value, jnp.where(down == over, spine, across))
+    return first, jnp.where(down < over, across, value)
 
 
 def wide_coded(piece, tile, value):
@@ -145,7 +192,7 @@
     owner_list,
     grads,
     stats,
-    fresh_out,
+    owner_terms,
     codes_out,
     owner_ref,
     own,
@@ -154,17 +201,13 @@
     sent,
     received,
     previous,
-    fresh,
-    packed,
     stat_codes,
     gathered,
     chosen,
     home_stat,
-    term,
     term_codes,
     terms_in,
     terms_out,
-    owner_terms,
     matrix,
     halves,
     band_codes,
@@ -188,6 +231,7 @@
     band_send,
     band_recv,
     out_sem,
+    own_sem,
 ):
     dp = lax.axis_index("dp")
     spot = lax.axis_index("expert")
@@ -199,8 +243,7 @@
     served = 2 * dp + slot
     own_band = band == dp
     tiles = extent // TILE
-    upper = [(a, b) for a in range(tiles) for b in range(a, tiles)]
-    depth = len(upper) * TILE // blocks
+    above, paired = pieces_of(tiles)
     half = extent // 2
 
     def block_of(turn, which):
@@ -233,21 +276,17 @@
         def _():
             tell(barrier, other, spot)
 
-    def rows_of(index):
-        return pl.ds(pl.multiple_of(index * depth, depth), depth)
+    def tile_at(index):
+        return slice(index * TILE, (index + 1) * TILE)
 
     stat_load.wait()
     for where in range(2):
-        for place, (a, b) in enumerate(upper):
-            packed[where, place * TILE : (place + 1) * TILE, :] = previous[
-                where, a * TILE : (a + 1) * TILE, b * TILE : (b + 1) * TILE
-            ]
-
-        @pl.loop(0, blocks)
-        def _(index):
-            codes, level = coded(packed[where, rows_of(index), :])
-            stat_codes[where, index, :depth, :] = codes
-            stat_codes[where, index, depth:, :] = as_note(level, NOTE)
+        put_pieces(
+            stat_codes.at[where],
+            lambda a, b, where=where: previous[where, tile_at(a), tile_at(b)],
+            tiles,
+            lambda index: None,
+        )
 
     @pl.when(jnp.logical_not(gate))
     def _():
@@ -377,18 +416,15 @@
 
     owner_load.wait()
     for index in range(blocks):
+        mine = jnp.logical_and(own_band, dp == index)
         chosen[index] = gathered[owner_ref[served * blocks + index]]
 
-    @pl.loop(0, blocks)
-    def _(index):
-        mine = jnp.logical_and(own_band, index == dp)
-
         @pl.when(jnp.logical_not(mine))
-        def _():
+        def _(index=index):
             to_home(index).start()
 
         @pl.when(mine)
-        def _():
+        def _(index=index):
             home_stat[index] = chosen[index]
 
     for copy, index, rows in (
@@ -415,17 +451,6 @@
     matrix[top, bottom] = corner
     matrix[top, top] = first
     matrix[bottom, bottom] = last
-    for place, (a, b) in enumerate(upper):
-        term[place * TILE : (place + 1) * TILE, :] = matrix[
-            a * TILE : (a + 1) * TILE, b * TILE : (b + 1) * TILE
-        ]
-
-    @pl.loop(0, blocks)
-    def _(index):
-        codes, level = coded(term[rows_of(index), :])
-        term_codes[index, :depth, :] = codes
-        term_codes[index, depth:, :] = as_note(level, NOTE)
-
     def to_server(index):
         return remote(
             term_codes.at[index],
@@ -446,9 +471,8 @@
             served,
         )
 
-    @pl.loop(0, blocks)
-    def _(index):
-        mine = jnp.logical_and(own_band, index == dp)
+    def send_term(index):
+        mine = jnp.logical_and(own_band, dp == index)
 
         @pl.when(jnp.logical_not(mine))
         def _():
@@ -457,6 +481,8 @@
         @pl.when(mine)
         def _():
             terms_in[index] = term_codes[index]
+
+    put_pieces(term_codes, lambda a, b: matrix[tile_at(a), tile_at(b)], tiles, send_term)
 
     @pl.loop(0, blocks)
     def _(index):
@@ -464,20 +490,19 @@
         def _():
             from_home(index).wait_recv()
 
-    for index in range(blocks):
-        packed[0, index * depth : (index + 1) * depth, :] = decoded(home_stat.at[index], depth)
-
     squares = jnp.zeros((1, 1), F32)
-    for place, (a, b) in enumerate(upper):
-        across = pl.ds(a * TILE, TILE), pl.ds(b * TILE, TILE)
-        piece = pl.ds(place * TILE, TILE)
-        value = DECAY * packed[0, piece, :] + GAIN / extent * term[piece, :]
-        if a == b:
-            value = value + jnp.where(diagonal(TILE, 0, TILE), F32(EPSILON), F32(0.0))
-        elif a // (tiles // 2) == b // (tiles // 2):
-            matrix[across[1], across[0]] = value.T
-        matrix[across[0], across[1]] = value
-        squares = squares + (1.0 if a == b else 2.0) * jnp.sum(value * value, keepdims=True)
+    damping = jnp.where(diagonal(TILE, 0, TILE), F32(EPSILON), F32(0.0))
+    for index, (a, b) in enumerate(above):
+        value = DECAY * piece_value(home_stat.at[index]) + GAIN / extent * matrix[tile_at(a), tile_at(b)]
+        matrix[tile_at(a), tile_at(b)] = value
+        if a // (tiles // 2) == b // (tiles // 2):
+            matrix[tile_at(b), tile_at(a)] = value.T
+        squares = squares + 2.0 * jnp.sum(value * value, keepdims=True)
+    for index, pair in enumerate(paired, len(above)):
+        for a, value in zip(pair, diagonal_tiles(home_stat.at[index])):
+            value = DECAY * value + GAIN / extent * matrix[tile_at(a), tile_at(a)] + damping
+            matrix[tile_at(a), tile_at(a)] = value
+            squares = squares + jnp.sum(value * value, keepdims=True)
 
     scaling = 2.5 * lax.rsqrt(squares)
     start = jnp.sqrt(jnp.sqrt(scaling))
@@ -497,6 +522,8 @@
     factor.put_symmetric(strips, *scaled)
     result.put_symmetric(strips, *[start * block for block in scaled])
 
+    keep_term = pltpu.make_async_copy(terms_out.at[spot], owner_terms.at[slot, band], own_sem)
+
     def spread_terms():
         @pl.loop(0, blocks)
         def _(index):
@@ -507,8 +534,7 @@
         terms_in[blocks] = jnp.zeros(terms_in.shape[1:], jnp.int16)
         owners = [owner_ref[served * blocks + index] for index in range(blocks)]
 
-        @pl.loop(0, experts)
-        def _(owner):
+        def spread_to(owner):
             at = jnp.int32(blocks)
             for index in range(blocks):
                 at = jnp.where(owners[index] == owner, index, at)
@@ -516,9 +542,12 @@
 
         @pl.loop(1, experts)
         def _(step):
-            to_owner(lax.rem(spot + step, experts)).start()
-
-        owner_terms[slot, band] = terms_out[spot]
+            other = lax.rem(spot + step, experts)
+            spread_to(other)
+            to_owner(other).start()
+
+        spread_to(spot)
+        keep_term.start()
 
     def to_owner(other):
         return remote(
@@ -603,21 +632,6 @@
     def _(step):
         from_owner(lax.rem(spot + step, experts)).wait_recv()
 
-    stores = []
-    for where in range(2):
-        for index in range(blocks):
-            packed[where, index * depth : (index + 1) * depth, :] = decoded(
-                owner_terms.at[where, index], depth
-            )
-        for place, (a, b) in enumerate(upper):
-            value = GAIN / extent * packed[where, place * TILE : (place + 1) * TILE, :]
-            down, over = pl.ds(a * TILE, TILE), pl.ds(b * TILE, TILE)
-            fresh[where, down, over] = DECAY * previous[where, down, over] + value
-            if a != b:
-                fresh[where, over, down] = DECAY * previous[where, over, down] + value.T
-        stores.append(pltpu.make_async_copy(fresh.at[where], fresh_out.at[where], load_sem.at[where]))
-        stores[-1].start()
-
     for copy in crossing.values():
         copy.wait_send()
     for copy in (far_right, far_left, direct_right, direct_left, mixed_right, mixed_left):
@@ -643,25 +657,60 @@
         from_replica(other).wait_recv()
 
     keep.wait()
-    for copy in stores:
-        copy.wait()
-
-
-def finish(codes, fresh_in, fresh_out, precond_out, taken, passing, precond, load_sem, store_sem):
+    keep_term.wait()
+
+
+def finish(
+    codes,
+    terms,
+    stats,
+    fresh_out,
+    precond_out,
+    taken,
+    taken_terms,
+    previous,
+    precond,
+    load_sem,
+    store_sem,
+):
+    load_terms = pltpu.make_async_copy(terms, taken_terms, load_sem.at[3])
+    load_terms.start()
+    loads = [
+        pltpu.make_async_copy(stats.at[where], previous.at[where], load_sem.at[where])
+        for where in range(2)
+    ]
+    loads[0].start()
     load_codes = pltpu.make_async_copy(codes, taken, load_sem.at[2])
     load_codes.start()
-    loads = [
-        pltpu.make_async_copy(fresh_in.at[where], passing.at[where], load_sem.at[where])
-        for where in range(2)
-    ]
-    for load in loads:
-        load.start()
+    loads[1].start()
     blocks, width, extent = precond.shape
     tiles = extent // TILE
     inner = tiles * width
+    above, paired = pieces_of(tiles)
     stores = []
-    load_codes.wait()
+
+    def store(src, dst, index):
+        stores.append(pltpu.make_async_copy(src, dst, store_sem.at[index]))
+        stores[-1].start()
+
+    load_terms.wait()
     for part in range(2):
+        loads[part].wait()
+
+        def add(a, b, value, part=part):
+            down, over = pl.ds(a * TILE, TILE), pl.ds(b * TILE, TILE)
+            previous[part, down, over] = DECAY * previous[part, down, over] + GAIN / extent * value
+
+        for index, (a, b) in enumerate(above):
+            value = piece_value(taken_terms.at[part, index])
+            add(a, b, value)
+            add(b, a, value.T)
+        for index, pair in enumerate(paired, len(above)):
+            for a, value in zip(pair, diagonal_tiles(taken_terms.at[part, index])):
+                add(a, a, value)
+        store(previous.at[part], fresh_out.at[part], part)
+        if part == 0:
+            load_codes.wait()
         for index in range(part * blocks // 2, (part + 1) * blocks // 2):
             levels = floats(taken[index, inner:, :])
             for tile in range(tiles):
@@ -670,17 +719,9 @@
                     taken[index, tile * width : (tile + 1) * width, :]
                 ) * step_of(levels[line : line + 1, :])
         here = pl.ds(part * blocks // 2, blocks // 2)
-        stores.append(
-            pltpu.make_async_copy(precond.at[here], precond_out.at[here], store_sem.at[2 + part])
-        )
-        stores[-1].start()
-        loads[part].wait()
-        stores.append(
-            pltpu.make_async_copy(passing.at[part], fresh_out.at[part], store_sem.at[part])
-        )
-        stores[-1].start()
-    for store in stores:
-        store.wait()
+        store(precond.at[here], precond_out.at[here], 2 + part)
+    for copy in stores:
+        copy.wait()
 
 
 def per_device(grad_parts, stat_owned, owner_list):
@@ -689,19 +730,17 @@
     partials, previous = grad_parts[0], stat_owned[0]
     extent = partials.shape[1]
     tiles = extent // TILE
-    packed_rows = tiles * (tiles + 1) // 2 * TILE
-    depth = packed_rows // blocks
     half = extent // 2
     dma = pltpu.SemaphoreType.DMA
     square = (extent, extent)
     width = extent // blocks
     inner = tiles * width + NOTE
-    piece = (depth + NOTE, TILE)
+    piece = (TILE + NOTE, TILE)
     message = tiles * (half + half // 2) + NOTE
     terms, codes = pl.pallas_call(
         functools.partial(kernel, extent, blocks, experts),
         out_shape=[
-            jax.ShapeDtypeStruct(previous.shape, F32),
+            jax.ShapeDtypeStruct((2, blocks, *piece), jnp.int16),
             jax.ShapeDtypeStruct((blocks, inner, TILE), jnp.int16),
         ],
         in_specs=[pl.BlockSpec(memory_space=pl.ANY)] * 3,
@@ -714,17 +753,13 @@
             pltpu.VMEM((6, message, TILE), jnp.int16),
             pltpu.VMEM((6, message, TILE), jnp.int16),
             pltpu.VMEM((2, *square), F32),
-            pltpu.VMEM((2, *square), F32),
-            pltpu.VMEM((2, packed_rows, TILE), F32),
             pltpu.VMEM((2, blocks, *piece), jnp.int16),
             pltpu.VMEM((experts, *piece), jnp.int16),
             pltpu.VMEM((blocks, *piece), jnp.int16),
             pltpu.VMEM((blocks, *piece), jnp.int16),
-            pltpu.VMEM((packed_rows, TILE), F32),
             pltpu.VMEM((blocks, *piece), jnp.int16),
             pltpu.VMEM((blocks + 1, *piece), jnp.int16),
             pltpu.VMEM((experts, *piece), jnp.int16),
-            pltpu.VMEM((2, blocks, *piece), jnp.int16),
             pltpu.VMEM(square, F32),
             pltpu.VMEM((10, *square), BF16),
             pltpu.VMEM((blocks, inner, TILE), jnp.int16),
@@ -748,6 +783,7 @@
             dma((blocks,)),
             dma((blocks,)),
             dma(()),
+            dma(()),
         ],
         compiler_params=pltpu.CompilerParams(
             collective_id=0, has_side_effects=True, vmem_limit_bytes=60 * 2**20
@@ -759,17 +795,18 @@
             jax.ShapeDtypeStruct(previous.shape, F32),
             jax.ShapeDtypeStruct((blocks, width, extent), F32),
         ],
-        in_specs=[pl.BlockSpec(memory_space=pl.ANY)] * 2,
+        in_specs=[pl.BlockSpec(memory_space=pl.ANY)] * 3,
         out_specs=[pl.BlockSpec(memory_space=pl.ANY)] * 2,
         scratch_shapes=[
             pltpu.VMEM(codes.shape, jnp.int16),
+            pltpu.VMEM(terms.shape, jnp.int16),
             pltpu.VMEM(previous.shape, F32),
             pltpu.VMEM((blocks, width, extent), F32),
-            dma((3,)),
+            dma((4,)),
             dma((4,)),
         ],
         compiler_params=pltpu.CompilerParams(vmem_limit_bytes=60 * 2**20),
-    )(codes, terms)
+    )(codes, terms, previous)
     return (fresh[None], precond)
 
 

time: 75.5 us -> 71.2 us (0.943)
  the two profiles are of different devices: /device:TPU:7 before, /device:TPU:25 now
where the time goes in v4:
time: 71.2 us; the launch traced here: 70.1 us
  Pallas kernels  69.3 us (97%)
  between operations  0.82 us (1%)
    pallas_call x1, Pallas kernels, per_device(): pl.pallas_call(functools.partial(kernel, extent, blocks, experts), out_sh...  65.9 us
    pallas_call x1, Pallas kernels, per_device(): pl.pallas_call(finish, out_shape=[jax.ShapeDtypeStruct(previous.shape, F3...  3.37 us

profile of v4, /device:TPU:25, one launch (start us, length us, event | category | flops | bytes accessed | tf_op | source)
XLA Modules:
  0.0 70.1 jit_solution(11425656799636833852)
XLA Ops:
  0.6 65.9 %shard_map.50 = (s16[2,8,144,128]{3,2,1,0:T(8,128)(2,1)}, s16[8,272,128]{2,1,0:T(8,128)(2,1)}) custom-call(s32[128]{0:T(128)} %owner_list.1, bf16[8,512,512]{2,1,0:T(8,128)(2,1)} %bitcast.5, f32[2,512,512]{2,1,0:T(8,128)} %bitcast.3), custom_call_target="tpu_custom_call" | custom-call | tf_op jit(solution)/shard_map/pallas_call | solution.py:740
  66.6 3.4 %shard_map.51 = (f32[2,512,512]{2,1,0:T(8,128)}, f32[8,64,512]{2,1,0:T(8,128)}) custom-call(s16[8,272,128]{2,1,0:T(8,128)(2,1)} %get-tuple-element.6.codes, s16[2,8,144,128]{3,2,1,0:T(8,128)(2,1)} %get-tuple-element.7.terms, f32[2,512,512]{2,1,0:T(8,128)} %bitcast.4), custom_call_target="tpu_custom_call" | custom-call | tf_op jit(solution)/shard_map/pallas_call | solution.py:792

commit v5 on v4

--- a/solution.py
+++ b/solution.py
@@ -276,18 +276,6 @@
         def _():
             tell(barrier, other, spot)
 
-    def tile_at(index):
-        return slice(index * TILE, (index + 1) * TILE)
-
-    stat_load.wait()
-    for where in range(2):
-        put_pieces(
-            stat_codes.at[where],
-            lambda a, b, where=where: previous[where, tile_at(a), tile_at(b)],
-            tiles,
-            lambda index: None,
-        )
-
     @pl.when(jnp.logical_not(gate))
     def _():
         pl.semaphore_wait(barrier, blocks - 1)
@@ -312,6 +300,18 @@
             spot,
         )
         crossing[turn].start()
+
+    def tile_at(index):
+        return slice(index * TILE, (index + 1) * TILE)
+
+    stat_load.wait()
+    for where in range(2):
+        put_pieces(
+            stat_codes.at[where],
+            lambda a, b, where=where: previous[where, tile_at(a), tile_at(b)],
+            tiles,
+            lambda index: None,
+        )
 
     def pair_sum(turn, rows, columns):
         return own[turn, rows, columns].astype(F32) + part[turn, rows, columns].astype(F32)

time: 71.2 us -> 71.7 us (level)
  the two profiles are of different devices: /device:TPU:25 before, /device:TPU:13 now
where the time goes in v5:
time: 71.7 us; the launch traced here: 71.6 us
  Pallas kernels  70.8 us (99%)
  between operations  0.82 us (1%)
    pallas_call x1, Pallas kernels, per_device(): pl.pallas_call(functools.partial(kernel, extent, blocks, experts), out_sh...  67.4 us
    pallas_call x1, Pallas kernels, per_device(): pl.pallas_call(finish, out_shape=[jax.ShapeDtypeStruct(previous.shape, F3...  3.37 us

profile of v5, /device:TPU:13, one launch (start us, length us, event | category | flops | bytes accessed | tf_op | source)
XLA Modules:
  0.0 71.6 jit_solution(16789251938593049841)
XLA Ops:
  0.6 67.4 %shard_map.50 = (s16[2,8,144,128]{3,2,1,0:T(8,128)(2,1)}, s16[8,272,128]{2,1,0:T(8,128)(2,1)}) custom-call(s32[128]{0:T(128)} %owner_list.1, bf16[8,512,512]{2,1,0:T(8,128)(2,1)} %bitcast.5, f32[2,512,512]{2,1,0:T(8,128)} %bitcast.3), custom_call_target="tpu_custom_call" | custom-call | tf_op jit(solution)/shard_map/pallas_call | solution.py:740
  68.0 3.4 %shard_map.51 = (f32[2,512,512]{2,1,0:T(8,128)}, f32[8,64,512]{2,1,0:T(8,128)}) custom-call(s16[8,272,128]{2,1,0:T(8,128)(2,1)} %get-tuple-element.6.codes, s16[2,8,144,128]{3,2,1,0:T(8,128)(2,1)} %get-tuple-element.7.terms, f32[2,512,512]{2,1,0:T(8,128)} %bitcast.4), custom_call_target="tpu_custom_call" | custom-call | tf_op jit(solution)/shard_map/pallas_call | solution.py:792

commit v6 on v4

--- a/solution.py
+++ b/solution.py
@@ -340,6 +340,39 @@
     crossing[2].wait_recv()
     far_right = pass_on(0, right, 2, top)
     far_left = pass_on(1, left, 2, bottom)
+    def to_plane(other):
+        return remote(
+            stat_codes.at[lax.rem(other, 2), other // 2],
+            gathered.at[spot],
+            plane_send.at[other],
+            plane_recv.at[spot],
+            dp,
+            other,
+        )
+
+    def from_plane(other):
+        return remote(
+            stat_codes.at[0, 0], gathered.at[other], plane_send.at[other], plane_recv.at[other], dp, other
+        )
+
+    @pl.when(gate)
+    def _():
+        pl.semaphore_wait(barrier, experts - 1)
+
+        @pl.loop(1, blocks)
+        def _(step):
+            tell(open_sem, step, spot)
+
+    @pl.when(jnp.logical_not(gate))
+    def _():
+        pl.semaphore_wait(open_sem, 1)
+
+    @pl.loop(1, experts)
+    def _(step):
+        to_plane(lax.rem(spot + step, experts)).start()
+
+    gathered[spot] = stat_codes[slot, band]
+
     loads[1].wait()
     crossing[1].wait_recv()
     direct_right = pass_on(2, right, 1, bottom)
@@ -347,38 +380,6 @@
     crossing[3].wait_recv()
     direct_left = pass_on(3, left, 3, top)
 
-    def to_plane(other):
-        return remote(
-            stat_codes.at[lax.rem(other, 2), other // 2],
-            gathered.at[spot],
-            plane_send.at[other],
-            plane_recv.at[spot],
-            dp,
-            other,
-        )
-
-    def from_plane(other):
-        return remote(
-            stat_codes.at[0, 0], gathered.at[other], plane_send.at[other], plane_recv.at[other], dp, other
-        )
-
-    @pl.when(gate)
-    def _():
-        pl.semaphore_wait(barrier, experts - 1)
-
-        @pl.loop(1, blocks)
-        def _(step):
-            tell(open_sem, step, spot)
-
-    @pl.when(jnp.logical_not(gate))
-    def _():
-        pl.semaphore_wait(open_sem, 1)
-
-    @pl.loop(1, experts)
-    def _(step):
-        to_plane(lax.rem(spot + step, experts)).start()
-
-    gathered[spot] = stat_codes[slot, band]
 
     loads[0].wait()
     crossing[0].wait_recv()

time: 71.2 us -> 71.2 us (level)
  no operation moved by 1% of the time
where the time goes in v6:
time: 71.2 us; the launch traced here: 70.1 us
  Pallas kernels  69.3 us (97%)
  between operations  0.82 us (1%)
    pallas_call x1, Pallas kernels, per_device(): pl.pallas_call(functools.partial(kernel, extent, blocks, experts), out_sh...  65.9 us
    pallas_call x1, Pallas kernels, per_device(): pl.pallas_call(finish, out_shape=[jax.ShapeDtypeStruct(previous.shape, F3...  3.37 us

profile of v6, /device:TPU:25, one launch (start us, length us, event | category | flops | bytes accessed | tf_op | source)
XLA Modules:
  0.0 70.1 jit_solution(4260579060787108459)
XLA Ops:
  0.6 65.9 %shard_map.50 = (s16[2,8,144,128]{3,2,1,0:T(8,128)(2,1)}, s16[8,272,128]{2,1,0:T(8,128)(2,1)}) custom-call(s32[128]{0:T(128)} %owner_list.1, bf16[8,512,512]{2,1,0:T(8,128)(2,1)} %bitcast.5, f32[2,512,512]{2,1,0:T(8,128)} %bitcast.3), custom_call_target="tpu_custom_call" | custom-call | tf_op jit(solution)/shard_map/pallas_call | solution.py:741
  66.6 3.4 %shard_map.51 = (f32[2,512,512]{2,1,0:T(8,128)}, f32[8,64,512]{2,1,0:T(8,128)}) custom-call(s16[8,272,128]{2,1,0:T(8,128)(2,1)} %get-tuple-element.6.codes, s16[2,8,144,128]{3,2,1,0:T(8,128)(2,1)} %get-tuple-element.7.terms, f32[2,512,512]{2,1,0:T(8,128)} %bitcast.4), custom_call_target="tpu_custom_call" | custom-call | tf_op jit(solution)/shard_map/pallas_call | solution.py:793
